TPU v7x, 128 devices: a whole 4x4x4 slice. The times are simulated.
128 devices in a mesh: wide: 16 (over z, y_hi, core), narrow: 8 (over y_lo, x).
Axes of the slice: x: 4, y: 4 (y_hi: 2, y_lo: 2; y = y_hi * 2 + y_lo), z: 4, core: 2. Of those that a mesh axis runs over, the one named last changes fastest.
Arguments:
- residual_in: bfloat16 [512, 18432], P('wide', 'narrow'), may hold values from -80 to 80
- query: bfloat16 [512, 12288], P('narrow', 'wide'), may hold values from -12 to 12
- cache: bfloat16 [8, 64, 1536, 512], P('narrow', 'wide'), may hold values from -200 to 200
- lengths: int32 [8, 64], P('narrow', 'wide'), may hold values from 2 to 1536, as said below
- gate_weight: bfloat16 [18432, 18432], P('narrow', 'wide'), may hold values from -0.046875 to 0.046875
- up_weight: bfloat16 [18432, 18432], P('narrow', 'wide'), may hold values from -0.046875 to 0.046875
- down_weight: bfloat16 [18432, 18432], P('wide', 'narrow'), may hold values from -0.046875 to 0.046875
- out_weight: bfloat16 [12288, 18432], P('wide', 'narrow'), may hold values from -0.21875 to 0.21875
Outputs:
- update: bfloat16 [512, 18432], P('wide', 'narrow')
Inputs may be any that keep to these rules, and one draw needn't show every extreme that they name: `lengths`: some row's length is exactly 1536.
All inputs are finite; a program needn't handle non-finite values.
Results may differ from a plain program's by a relative error of at most 0.0062.
Values may be sent and summed in bfloat16 or wider, within the bound.
A program may use at most 128 MiB of HBM per device.

v0:
```python
import math

import jax
import jax.numpy as jnp
from jax import lax
from jax.sharding import PartitionSpec as P

HEADS = 48
HEAD = 256


def local(residual_in, query, cache, lengths, gate_weight, up_weight, down_weight, out_weight):
    rows_f = residual_in.astype(jnp.float32)
    full_width = residual_in.shape[1] * lax.axis_size("narrow")
    totals, squares = lax.psum(
        (jnp.sum(rows_f, axis=1), jnp.sum(rows_f * rows_f, axis=1)), "narrow"
    )
    mean = (totals / full_width)[:, None]
    variance = (squares / full_width)[:, None] - mean * mean
    normed = ((rows_f - mean) * lax.rsqrt(variance + 1e-06)).astype(jnp.bfloat16)
    piece = lax.all_gather(normed, "wide", axis=0, tiled=True)
    gate_piece = jnp.dot(piece, gate_weight, preferred_element_type=jnp.float32)
    up_piece = jnp.dot(piece, up_weight, preferred_element_type=jnp.float32)
    partial_value = jnp.concatenate([gate_piece, up_piece], axis=1)
    hidden_width = gate_weight.shape[1]
    summed = lax.psum(partial_value, "narrow")
    hidden = (jax.nn.silu(summed[:, :hidden_width]) * summed[:, hidden_width:]).astype(jnp.bfloat16)
    ffn_part = jnp.dot(hidden, down_weight, preferred_element_type=jnp.float32)
    query_local = lax.all_to_all(query, "wide", split_axis=0, concat_axis=1, tiled=True)
    row_count = query_local.shape[0]
    query_heads = query_local.reshape(row_count, HEADS, HEAD)
    local_cache = cache[0]
    keys = local_cache[:, :, :HEAD]
    values = local_cache[:, :, HEAD:]
    scores = jnp.einsum(
        "rhe,rte->rht", query_heads, keys, preferred_element_type=jnp.float32
    ) / math.sqrt(HEAD)
    valid = jnp.arange(local_cache.shape[1])[None, None, :] < lengths[0][:, None, None]
    scores = jnp.where(valid, scores, -jnp.inf)
    top = jnp.max(scores, axis=2, keepdims=True)
    weights = jnp.exp(scores - top)
    probs = (weights / jnp.sum(weights, axis=2, keepdims=True)).astype(jnp.bfloat16)
    context = jnp.einsum("rht,rte->rhe", probs, values, preferred_element_type=jnp.float32)
    context = context.astype(jnp.bfloat16).reshape(row_count, HEADS * HEAD)
    context_local = lax.all_to_all(context, "wide", split_axis=1, concat_axis=0, tiled=True)
    attn_part = jnp.dot(
        lax.all_gather(context_local, "narrow", axis=0, tiled=True),
        out_weight,
        preferred_element_type=jnp.float32,
    )
    ffn_total = lax.psum_scatter(ffn_part, "wide", scatter_dimension=0, tiled=True)
    attn_total = lax.psum_scatter(attn_part, "wide", scatter_dimension=0, tiled=True)
    update = ffn_total + attn_total
    return update.astype(jnp.bfloat16)


def solution(mesh):
    return jax.shard_map(
        local,
        mesh=mesh,
        in_specs=(
            P("wide", "narrow"),
            P("narrow", "wide"),
            P("narrow", "wide", None, None),
            P("narrow", "wide"),
            P("narrow", "wide"),
            P("narrow", "wide"),
            P("wide", "narrow"),
            P("wide", "narrow"),
        ),
        out_specs=P("wide", "narrow"),
        check_vma=False,
    )
```

profile of v0, /device:TPU:0, one launch (start us, length us, event | category | flops | bytes accessed | tf_op | source)
XLA Modules:
  0.0 341.8 jit_solution(15260796573985668706)
XLA Ops:
  6.5 0.0 copy-start
  6.5 1.2 convert_reduce_fusion
  7.7 19.8 %all-reduce = (f32[32]{0:T(128)S(1)}, f32[32]{0:T(128)S(1)}) all-reduce(f32[32]{0:T(128)S(1)} %get-tuple-element.6, f32[32]{0:T(128)S(1)} %get-tuple-element.5), channel_id=1, replica_groups=mesh['wide'=16,'narrow'=8] {'narrow'}, use_global_device_ids=true, to_apply=%region_3.0 | all-reduce | flops 64 | bytes 512 | tf_op jit(solution)/shard_map/psum | solution.py:15
  27.6 1.7 fusion.22
  29.2 0.0 all-gather.2.cloned.1.call-update
  29.3 0.0 all-reduce.3.cloned.1.call-start
  29.3 48.2 %all-gather.2.cloned.1.call-done = bf16[512,2304]{1,0:T(8,128)(2,1)} async-done(((bf16[32,2304]{1,0:T(8,128)(2,1)}), bf16[512,2304]{1,0:T(8,128)(2,1)}) %all-gather.2.cloned.1.call-update) | async-done | bytes 2359312 | tf_op jit(solution)/shard_map/all_gather | solution.py:21
  77.5 6.6 %fusion.27 = f32[512,1152]{1,0:T(8,128)S(1)} fusion(bf16[512,2304]{1,0:T(8,128)(2,1)} %all-gather.2.cloned.1.call-done, bf16[2304,1152]{1,0:T(8,128)(2,1)} %param.12), kind=kOutput, calls=%fused_computation.30 | convolution fusion | flops 2717908992 | bytes 10027008 | tf_op jit(solution)/shard_map/dot_general | solution.py:22
  84.1 5.8 %fusion.28 = f32[512,1152]{1,0:T(8,128)S(1)} fusion(bf16[512,2304]{1,0:T(8,128)(2,1)S(1)} %copy-done.4, bf16[2304,1152]{1,0:T(8,128)(2,1)} %param.13), kind=kOutput, calls=%fused_computation.31 | convolution fusion | flops 2717908992 | bytes 10027008 | tf_op jit(solution)/shard_map/dot_general | solution.py:23
  89.9 2.5 pad_maximum_fusion
  92.4 0.0 all-reduce.3.cloned.1.call-update
  92.4 1.6 all_to_all.26
  94.0 4.2 %all-to-all-start = ((bf16[16,4,768]{2,1,0:T(4,128)(2,1)}), bf16[16,4,768]{2,1,0:T(4,128)(2,1)}, u32[]{:S(2)}, u32[]{:S(2)}) async-start(bf16[16,4,768]{2,1,0:T(4,128)(2,1)} %all_to_all.26), calls=%async_computation | async-start | bytes 196608 | tf_op jit(solution)/shard_map/all_to_all | solution.py:29
  98.2 0.0 reduce-scatter.2.cloned.1.call-start
  98.2 0.1 iota_compare_fusion
  98.3 7.7 %all-to-all-done = bf16[16,4,768]{2,1,0:T(4,128)(2,1)} async-done(((bf16[16,4,768]{2,1,0:T(4,128)(2,1)}), bf16[16,4,768]{2,1,0:T(4,128)(2,1)}, u32[]{:S(2)}, u32[]{:S(2)}) %all-to-all-start) | async-done | bytes 98336 | tf_op jit(solution)/shard_map/all_to_all | solution.py:29
  106.0 1.5 copy.12
  107.5 1.6 reshape.44
  109.1 3.0 fusion.9
  112.2 1.0 copy-done.1
  113.2 0.3 fusion.26
  113.5 4.0 %fusion.17 = bf16[4,48,256]{2,1,0:T(8,128)(2,1)} fusion(bf16[4,1536,512]{2,1,0:T(8,128)(2,1)} %bitcast.15, f32[4,48]{1,0:T(4,128)S(1)} %fusion.26, f32[4,48,1536]{2,1,0:T(8,128)} %copy-done.1), kind=kOutput, calls=%fused_computation.16 | convolution fusion | flops 151930560 | bytes 5604096 | tf_op jit(solution)/shard_map/rht,rte->rhe/dot_general | solution.py:43
  117.5 1.6 all_to_all.29
  119.1 0.9 copy.13
  120.1 33.2 %all_to_all.35 = bf16[4,16,768]{2,0,1:T(4,128)(2,1)} all-to-all(bf16[4,16,768]{2,0,1:T(4,128)(2,1)S(1)} %copy.13), channel_id=1, replica_groups=mesh['wide'=16,'narrow'=8] {'wide'}, dimensions={1} | all-to-all | bytes 196608 | tf_op jit(solution)/shard_map/all_to_all | solution.py:45
  153.2 1.6 all_to_all.32
  154.8 86.2 %all_gather.7 = bf16[512,768]{1,0:T(8,128)(2,1)} all-gather(bf16[64,768]{1,0:T(8,128)(2,1)} %all_to_all.32), channel_id=1, replica_groups=mesh['wide'=16,'narrow'=8] {'narrow'}, dimensions={0}, use_global_device_ids=true | all-gather | bytes 884736 | tf_op jit(solution)/shard_map/all_gather | solution.py:47
  241.0 7.0 %fusion.14 = f32[512,2304]{1,0:T(8,128)S(1)} fusion(bf16[1152,2304]{1,0:T(8,128)(2,1)} %param.14, f32[512,2304]{1,0:T(8,128)} %all-reduce.3.cloned.1.call-done), kind=kOutput, calls=%fused_computation.13 | convolution fusion | flops 2721447936 | bytes 14745600 | tf_op jit(solution)/shard_map/dot_general | solution.py:28
  248.0 4.1 %convolution_add_fusion = f32[512,2304]{1,0:T(8,128)} fusion(f32[512,2304]{1,0:T(8,128)S(1)} %fusion.14, bf16[512,768]{1,0:T(8,128)(2,1)S(1)} %copy-done.2, bf16[768,2304]{1,0:T(8,128)(2,1)S(1)} %copy-done), kind=kOutput, calls=%fused_computation.1 | convolution fusion | flops 1813118976 | bytes 13762560 | tf_op jit(solution)/shard_map/dot_general | solution.py:46
  252.1 0.0 reduce-scatter.2.cloned.1.call-update
  252.2 81.5 %reduce-scatter.2.cloned.1.call-done = f32[32,2304]{1,0:T(8,128)} async-done(((f32[512,2304]{1,0:T(8,128)}), f32[32,2304]{1,0:T(8,128)}) %reduce-scatter.2.cloned.1.call-update) | async-done | bytes 294928 | tf_op jit(solution)/shard_map/reduce_scatter | solution.py:51
  333.7 1.6 convert_element_type.23
  (11 shorter events, 0.0 us)
Async XLA Ops:
  6.5 241.5 %copy-start = (bf16[768,2304]{1,0:T(8,128)(2,1)S(1)}, bf16[768,2304]{1,0:T(8,128)(2,1)}, u32[]{:S(2)}) copy-start(bf16[768,2304]{1,0:T(8,128)(2,1)} %param.15) | copy-start | bytes 10616836
  6.5 71.0 %all-gather.2.cloned.1.call-start = ((), (), s32[]{:S(2)}) async-start(), calls=%async_computation.3 | async-start | bytes 2506752 | tf_op jit(solution)/shard_map/all_gather | solution.py:21
  29.3 211.7 %all-reduce.3.cloned.1.call-start = ((), (), s32[]{:S(2)}) async-start(), calls=%async_computation.4 | async-start | bytes 9437184 | tf_op jit(solution)/shard_map/psum | solution.py:26
  77.5 6.6 %copy-start.4 = (bf16[512,2304]{1,0:T(8,128)(2,1)S(1)}, bf16[512,2304]{1,0:T(8,128)(2,1)}, u32[]{:S(2)}) copy-start(bf16[512,2304]{1,0:T(8,128)(2,1)} %all-gather.2.cloned.1.call-done) | copy-start | bytes 7077892
  92.4 5.8 %copy-start.3 = (s32[1,4]{1,0:T(1,128)S(1)}, s32[1,4]{1,0:T(1,128)}, u32[]{:S(2)}) copy-start(s32[1,4]{1,0:T(1,128)} %param.11) | copy-start | bytes 52
  94.0 12.0 %all-to-all-start = ((bf16[16,4,768]{2,1,0:T(4,128)(2,1)}), bf16[16,4,768]{2,1,0:T(4,128)(2,1)}, u32[]{:S(2)}, u32[]{:S(2)}) async-start(bf16[16,4,768]{2,1,0:T(4,128)(2,1)} %all_to_all.26), calls=%async_computation | async-start | bytes 196608 | tf_op jit(solution)/shard_map/all_to_all | solution.py:29
  98.2 235.5 %reduce-scatter.2.cloned.1.call-start = ((), (), s32[]{:S(2)}) async-start(), calls=%async_computation.5 | async-start | bytes 5013504 | tf_op jit(solution)/shard_map/reduce_scatter | solution.py:51
  112.2 1.0 copy-start.1
  241.0 7.0 %copy-start.2 = (bf16[512,768]{1,0:T(8,128)(2,1)S(1)}, bf16[512,768]{1,0:T(8,128)(2,1)}, u32[]{:S(2)}) copy-start(bf16[512,768]{1,0:T(8,128)(2,1)} %all_gather.7) | copy-start | bytes 2359300
Sparse Core Ops, SparseCore 0:
  29.4 48.1 all-gather.1
  92.6 113.7 all-reduce.2
  252.3 81.3 reduce-scatter.1
where the time goes:
time: 342 us
  blocking collectives  139 us (41%)
  waiting for transfers between devices  137 us (40%)
  matrix products  30.5 us (9%)
  between operations  13.2 us (4%)
  local copies, waits for them, and re-layouts  9.77 us (3%)
  other arithmetic  7.46 us (2%)
  starting transfers between devices  4.24 us (1%)
    all_gather x1, blocking collectives, local(): lax.all_gather(context_local, 'narrow', axis=0, tiled=True)  86.2 us
    reduce_scatter x1, waiting for transfers between devices, local(): lax.psum_scatter(ffn_part, 'wide', scatter_dimension=0, tiled=True)  81.5 us
    all_gather x1, waiting for transfers between devices, local(): piece = lax.all_gather(normed, 'wide', axis=0, tiled=True)  48.2 us
    all_to_all x1, blocking collectives, local(): lax.all_to_all(context, 'wide', split_axis=1, concat_axis=0, tiled=True)  33.2 us
    psum x1, blocking collectives, local(): lax.psum((jnp.sum(rows_f, axis=1), jnp.sum(rows_f * rows_f, axis=1)), 'na...  19.8 us
    all_to_all x1, waiting for transfers between devices, local(): lax.all_to_all(query, 'wide', split_axis=0, concat_axis=1, tiled=True)  7.69 us
    dot_general x1, matrix products, local(): ffn_part = jnp.dot(hidden, down_weight, preferred_element_type=jnp.float32)  6.98 us
  transfers between devices with their start and end apart: 4, of which 3 were waited for; matrix products, arithmetic and copies ran while one was open for 3% of the time, Pallas kernels for 0%

commit v1 on v0

v1 whole, which is shorter than its diff:
```python
import jax
import jax.numpy as jnp
from jax import lax
from jax.experimental import pallas as pl
from jax.experimental.pallas import tpu as pltpu
from jax.sharding import PartitionSpec as P

HEADS = 48
HEAD = 256
MESH = pl.DeviceIdType.MESH
BF = jnp.bfloat16
F32 = jnp.float32
STEPS = (0, 1, 3, 2)


def dot(a, b):
    return jnp.dot(a, b, preferred_element_type=F32)


def pick(rows, cols, rule):
    i = lax.broadcasted_iota(jnp.int32, (rows, cols), 0)
    k = lax.broadcasted_iota(jnp.int32, (rows, cols), 1)
    return jnp.where(rule(i, k), 1.0, 0.0).astype(BF)


def kernel(
    res, query, lengths, cache_hbm, wg_hbm, wu_hbm, wd_hbm, wo_hbm, out,
    wgu, wd, wo, cache, xg, st, pb, rb, hid, ctxg, acc, cs, rc, se, rz, own, ys, ry,
    qs, qr, qh, cb, csd, crv, lsem, ssem, rsem,
):
    w = lax.axis_index("wide")
    n = lax.axis_index("narrow")
    z, yh, c = w // 4, (w // 2) % 2, w % 2
    yl, x = n // 4, n % 4
    width = res.shape[1] * 8
    half = wg_hbm.shape[1]
    taken = [0]

    def near(k):
        return ((yl + k // 4) % 2) * 4 + (x + k % 4) % 4

    def far(k):
        return ((z + k // 4) % 4) * 4 + ((yh + (k // 2) % 2) % 2) * 2 + (c + k % 2) % 2

    def send(src, dst, wt, nt):
        i = taken[0]
        taken[0] += 1
        copy = pltpu.make_async_remote_copy(
            src_ref=src, dst_ref=dst, send_sem=ssem.at[i], recv_sem=rsem.at[i],
            device_id=(wt, nt), device_id_type=MESH,
        )
        copy.start()
        return copy

    pw = z * 4 + (1 - yh) * 2 + c
    sw = z * 4 + yh * 2 + (1 - c)
    sent = []

    loads = []
    for i, (src, dst) in enumerate((
        (cache_hbm.at[0], cache),
        (wg_hbm, wgu.at[:, pl.ds(0, half)]),
        (wu_hbm, wgu.at[:, pl.ds(half, half)]),
        (wo_hbm, wo),
        (wd_hbm, wd),
    )):
        copy = pltpu.make_async_copy(src, dst, lsem.at[i])
        copy.start()
        loads.append(copy)

    barrier = pltpu.get_barrier_semaphore()
    for k in range(1, 8):
        pl.semaphore_signal(barrier, inc=1, device_id=(w, near(k)), device_id_type=MESH)
    for k in range(1, 16):
        pl.semaphore_signal(barrier, inc=1, device_id=(far(k), n), device_id_type=MESH)

    rows_f = res[...].astype(F32)
    total = jnp.sum(rows_f, axis=1, keepdims=True)
    square = jnp.sum(rows_f * rows_f, axis=1, keepdims=True)
    lane = lax.broadcasted_iota(jnp.int32, (32, 128), 1)
    mine = jnp.where(lane < 64, total, square)
    st[0] = mine
    moved = jnp.zeros((256, HEAD), F32)
    for h in range(3):
        table = pick(256, 64, lambda i, k: ((i >> 4) == (k >> 2)) & ((i & 15) == 4 * h + (k & 3)))
        moved += dot(table, query[:, h * HEAD:(h + 1) * HEAD])
    qs[...] = moved.astype(BF).reshape(16, 16, HEAD)
    pl.semaphore_wait(barrier, 22)

    stats = [send(st.at[0], st.at[k], w, near(k)) for k in range(1, 8)]
    queries = [send(qs.at[far(k)], qr.at[w], far(k), n) for k in range(1, 16)]
    qr[w] = qs[w]
    sent += stats + queries
    for k, copy in enumerate(stats):
        copy.wait_recv()
        mine += st[k + 1]
    mean = mine[:, 0:1] / width
    variance = mine[:, 64:65] / width - mean * mean
    xg[z, yh, c] = ((rows_f - mean) * lax.rsqrt(variance + 1e-06)).astype(BF)

    def rows_at(zz, yy):
        return xg.at[zz, yy, c]

    def z_at(d):
        return ((z + d) % 4) * 4 + yh * 2 + c

    mate = send(rows_at(z, yh), rows_at(z, yh), pw, n)
    sib = send(rows_at(z, yh), rows_at(z, yh), sw, n)
    first = {d: send(rows_at(z, yh), rows_at(z, yh), z_at(d), n) for d in (1, 3)}
    sent += [mate, sib, first[1], first[3]]

    for copy in queries:
        copy.wait_recv()
    table = pick(192, 256, lambda i, k: (i == (k & 3) * 48 + (k >> 4) * 3 + ((k >> 2) & 3)) & (((k >> 2) & 3) < 3))
    qh[...] = dot(table, qr[...].reshape(256, HEAD)).astype(BF)
    loads[0].wait()

    def attend(r):
        scores = lax.dot_general(
            qh[r * 48:(r + 1) * 48, :], cache[r, :, 0:HEAD], (((1,), (1,)), ((), ())),
            preferred_element_type=F32,
        ) * (1.0 / 16.0)
        spot = lax.broadcasted_iota(jnp.int32, scores.shape, 1)
        scores = jnp.where(spot < lengths[0, r], scores, -jnp.inf)
        top = jnp.max(scores, axis=1, keepdims=True)
        weights = jnp.exp(scores - top)
        probs = (weights / jnp.sum(weights, axis=1, keepdims=True)).astype(BF)
        cb[r * 48:(r + 1) * 48, :] = dot(probs, cache[r, :, HEAD:2 * HEAD]).astype(BF)

    attend(0)

    mate.wait_recv()
    psib = send(rows_at(z, 1 - yh), rows_at(z, 1 - yh), sw, n)
    second = {d: send(rows_at(z, 1 - yh), rows_at(z, 1 - yh), z_at(d), n) for d in (1, 3)}
    first[2] = send(rows_at(z, yh), rows_at(z, yh), z_at(2), n)
    second[2] = send(rows_at(z, 1 - yh), rows_at(z, 1 - yh), z_at(2), n)
    sent += [psib, *second.values(), first[2]]
    attend(1)

    passed = {}

    def hand_over(d):
        first[d].wait_recv()
        second[d].wait_recv()
        zc = (z + 4 - d) % 4
        passed[d] = send(xg.at[zc, :, c], xg.at[zc, :, c], sw, n)
        sent.append(passed[d])

    parts, hidden_parts, cores, zs = {}, {}, {}, {}

    def first_product(j):
        d = STEPS[j]
        zc = (z + 4 - d) % 4
        if d == 0:
            sib.wait_recv()
            psib.wait_recv()
            loads[1].wait()
            loads[2].wait()
        else:
            passed[d].wait_recv()
        rows = xg[zc].reshape(128, xg.shape[4])

        def tile(t, carry):
            cols = pl.ds(pl.multiple_of(t * 256, 256), 256)
            pb[j, :, :, cols] = dot(rows, wgu[:, cols]).astype(BF).reshape(8, 16, 256)
            return carry

        lax.fori_loop(0, wgu.shape[1] // 256, tile, 0)
        parts[j] = [send(pb.at[j, near(k)], rb.at[j, k], w, near(k)) for k in range(1, 8)]
        sent.extend(parts[j])

    def hidden_piece(j):
        summed = pb[j, n].astype(F32)
        for k in range(1, 8):
            parts[j][k - 1].wait_recv()
            summed += rb[j, k].astype(F32)
        gate, up = summed[:, :half], summed[:, half:]
        hid[j, n] = (gate / (1.0 + jnp.exp(-gate)) * up).astype(BF)
        hidden_parts[j] = [send(hid.at[j, n], hid.at[j, n], w, near(k)) for k in range(1, 8)]
        sent.extend(hidden_parts[j])

    def second_product(j):
        zc = (z + 4 - STEPS[j]) % 4
        for copy in hidden_parts[j]:
            copy.wait_recv()
        if j == 0:
            for copy in contexts:
                copy.wait_recv()
            loads[3].wait()
            loads[4].wait()
        rows = hid[j].reshape(128, half)
        heads = ctxg[pl.ds(2 * zc, 2)].reshape(128, ctxg.shape[2])
        slot = j % 2

        def tile(t, carry):
            cols = pl.ds(pl.multiple_of(t * 256, 256), 256)
            value = dot(rows, wd[:, cols]) + dot(heads, wo[:, cols])
            acc[slot, :, :, :, cols] = value.reshape(2, 2, 32, 256)
            return carry

        lax.fori_loop(0, wd.shape[1] // 256, tile, 0)
        cs[j] = acc[slot, :, 1 - c].astype(BF)
        cores[j] = send(cs.at[j], rc.at[j], sw, n)
        sent.append(cores[j])

    def core_sum(j):
        d = STEPS[j]
        cores[j].wait_recv()
        value = acc[j % 2, :, c] + rc[j].astype(F32)
        if d == 0:
            own[...] = value
        else:
            se[j] = value.astype(BF)
            e = 4 - d
            zs[e] = send(se.at[j], rz.at[e], z_at(e), n)
            sent.append(zs[e])

    first_product(0)
    hand_over(1)
    hand_over(3)
    attend(2)
    first_product(1)
    attend(3)
    table = pick(256, 192, lambda k, i: (i == (k & 3) * 48 + (k >> 4) * 3 + ((k >> 2) & 3)) & (((k >> 2) & 3) < 3))
    csd[...] = dot(table, cb[...]).astype(BF).reshape(16, 16, HEAD)
    turned = [send(csd.at[far(k)], crv.at[w], far(k), n) for k in range(1, 16)]
    crv[w] = csd[w]
    sent += turned
    hand_over(2)
    first_product(2)
    hidden_piece(0)
    first_product(3)
    for copy in turned:
        copy.wait_recv()
    arrived = crv[...].reshape(256, HEAD)
    for h in range(3):
        table = pick(64, 256, lambda i, k: ((k >> 4) == (i >> 2)) & ((k & 15) == 4 * h + (i & 3)))
        ctxg[n, :, h * HEAD:(h + 1) * HEAD] = dot(table, arrived).astype(BF)
    contexts = [send(ctxg.at[n], ctxg.at[n], w, near(k)) for k in range(1, 8)]
    sent += contexts
    hidden_piece(1)
    second_product(0)
    hidden_piece(2)
    core_sum(0)
    second_product(1)
    hidden_piece(3)
    core_sum(1)
    second_product(2)
    core_sum(2)
    second_product(3)
    core_sum(3)

    def finished(b):
        value = own[b]
        for e in (3, 1, 2):
            value += rz[e, b].astype(F32)
        return value

    for e in (3, 1, 2):
        zs[e].wait_recv()
    ys[...] = finished(1 - yh).astype(BF)
    last = send(ys, ry, pw, n)
    sent.append(last)
    value = finished(yh)
    for copy in sent:
        copy.wait_send()
    last.wait_recv()
    out[...] = (value + ry[...].astype(F32)).astype(BF)


def local(residual_in, query, cache, lengths, gate_weight, up_weight, down_weight, out_weight):
    rows, width = residual_in.shape
    half = gate_weight.shape[1]
    cols = query.shape[1]
    places = cache.shape[2]
    vmem = pl.BlockSpec(memory_space=pltpu.VMEM)
    hbm = pl.BlockSpec(memory_space=pl.ANY)
    copies = 160
    return pl.pallas_call(
        kernel,
        out_shape=jax.ShapeDtypeStruct((rows, width), BF),
        in_specs=[vmem, vmem, pl.BlockSpec(memory_space=pltpu.SMEM), hbm, hbm, hbm, hbm, hbm],
        out_specs=vmem,
        scratch_shapes=[
            pltpu.VMEM((width, 2 * half), BF),
            pltpu.VMEM((half, width), BF),
            pltpu.VMEM((cols, width), BF),
            pltpu.VMEM((4, places, 2 * HEAD), BF),
            pltpu.VMEM((4, 2, 2, 32, width), BF),
            pltpu.VMEM((8, 32, 128), F32),
            pltpu.VMEM((4, 8, 16, 2 * half), BF),
            pltpu.VMEM((4, 8, 16, 2 * half), BF),
            pltpu.VMEM((4, 8, 16, half), BF),
            pltpu.VMEM((8, 64, cols), BF),
            pltpu.VMEM((2, 2, 2, 32, width), F32),
            pltpu.VMEM((4, 2, 32, width), BF),
            pltpu.VMEM((4, 2, 32, width), BF),
            pltpu.VMEM((4, 2, 32, width), BF),
            pltpu.VMEM((4, 2, 32, width), BF),
            pltpu.VMEM((2, 32, width), F32),
            pltpu.VMEM((32, width), BF),
            pltpu.VMEM((32, width), BF),
            pltpu.VMEM((16, 16, HEAD), BF),
            pltpu.VMEM((16, 16, HEAD), BF),
            pltpu.VMEM((192, HEAD), BF),
            pltpu.VMEM((192, HEAD), BF),
            pltpu.VMEM((16, 16, HEAD), BF),
            pltpu.VMEM((16, 16, HEAD), BF),
            pltpu.SemaphoreType.DMA((5,)),
            pltpu.SemaphoreType.DMA((copies,)),
            pltpu.SemaphoreType.DMA((copies,)),
        ],
        compiler_params=pltpu.CompilerParams(
            collective_id=0, has_side_effects=True, vmem_limit_bytes=58 << 20
        ),
        name="layer",
    )(residual_in, query, lengths, cache, gate_weight, up_weight, down_weight, out_weight)


def solution(mesh):
    return jax.shard_map(
        local,
        mesh=mesh,
        in_specs=(
            P("wide", "narrow"),
            P("narrow", "wide"),
            P("narrow", "wide", None, None),
            P("narrow", "wide"),
            P("narrow", "wide"),
            P("narrow", "wide"),
            P("wide", "narrow"),
            P("wide", "narrow"),
        ),
        out_specs=P("wide", "narrow"),
        check_vma=False,
    )
```

time: 342 us -> 107 us (0.31)
  blocking collectives: 139 us -> 0 us
  waiting for transfers between devices: 137 us -> 0 us
  Pallas kernels: 0 us -> 105 us
  matrix products: 30.5 us -> 0 us
  between operations: 13.2 us -> 0.01 us
  local copies, waits for them, and re-layouts: 9.77 us -> 1.58 us
  other arithmetic: 7.46 us -> 0 us
  starting transfers between devices: 4.24 us -> 0 us
    pallas_call x0 -> x1, Pallas kernels: none -> 105 us  [local(): pl.pallas_call(kernel, out_shape=jax.ShapeDtypeStruct((rows, width), BF),...]
    all_gather x1 -> x0, blocking collectives: 86.2 us -> none  [local(): lax.all_gather(context_local, 'narrow', axis=0, tiled=True)]
    reduce_scatter x1 -> x0, waiting for transfers between devices: 81.5 us -> none  [local(): lax.psum_scatter(ffn_part, 'wide', scatter_dimension=0, tiled=True)]
    all_gather x1 -> x0, waiting for transfers between devices: 48.2 us -> none  [local(): piece = lax.all_gather(normed, 'wide', axis=0, tiled=True)]
    all_to_all x1 -> x0, blocking collectives: 33.2 us -> none  [local(): lax.all_to_all(context, 'wide', split_axis=1, concat_axis=0, tiled=True)]
    dot_general x6 -> x0, matrix products: 30.5 us -> none  [the longest x1 6.98 us: local(): ffn_part = jnp.dot(hidden, down_weight, preferred_element_type=jnp.float32)]
    psum x1 -> x0, blocking collectives: 19.8 us -> none  [local(): lax.psum((jnp.sum(rows_f, axis=1), jnp.sum(rows_f * rows_f, axis=1)), 'na...]
    all_to_all x1 -> x0, waiting for transfers between devices: 7.69 us -> none  [local(): lax.all_to_all(query, 'wide', split_axis=0, concat_axis=1, tiled=True)]
  transfers between devices with their start and end apart: 4 -> 0, of which waited for: 3 -> 0; matrix products, arithmetic and copies ran while one was open for 3% -> 0% of each run, Pallas kernels for 0% -> 0%
where the time goes in v1:
time: 107 us
  Pallas kernels  105 us (98%)
  local copies, waits for them, and re-layouts  1.58 us (1%)
    pallas_call x1, Pallas kernels, local(): pl.pallas_call(kernel, out_shape=jax.ShapeDtypeStruct((rows, width), BF),...  105 us

profile of v1, /device:TPU:0, one launch (start us, length us, event | category | flops | bytes accessed | tf_op | source)
XLA Modules:
  0.0 106.8 jit_solution(6987132395150268743)
XLA Ops:
  0.0 105.2 %layer.1 = bf16[32,2304]{1,0:T(8,128)(2,1)} custom-call(bf16[32,2304]{1,0:T(8,128)(2,1)} %res.1, bf16[64,768]{1,0:T(8,128)(2,1)} %query.1, s32[1,4]{1,0:T(1,128)} %lengths.1, bf16[1,4,1536,512]{3,2,1,0:T(8,128)(2,1)} %cache_hbm.1, bf16[2304,1152]{1,0:T(8,128)(2,1)} %wg_hbm.1, bf16[2304,1152]{1,0:T(8,128)(2,1)} %wu_hbm.1, bf16[1152,2304]{1,0:T(8,128)(2,1)} %wd_hbm.1, ...), custom_call_target="tpu_custom_call" | custom-call | tf_op jit(solution)/shard_map/layer/pallas_call | solution.py:279
  105.2 1.6 %copy.10 = bf16[32,2304]{1,0:T(8,128)(2,1)} copy(bf16[32,2304]{1,0:T(8,128)(2,1)} %layer.1) | data formatting | bytes 294912

commit v2 on v0

v2 whole, which is shorter than its diff:
```python
import jax
import jax.numpy as jnp
from jax import lax
from jax.experimental import pallas as pl
from jax.experimental.pallas import tpu as pltpu
from jax.sharding import PartitionSpec as P

HEADS = 48
HEAD = 256
MESH = pl.DeviceIdType.MESH
BF = jnp.bfloat16
F32 = jnp.float32
STEPS = (1, 3, 2, 0)
DIMS = "aby"
ORDERS = ("aby", "bya", "yab")
WIDE = "abhc"
TURNS = "chab"


def whole(p):
    return 4 * (2 * ((p >> 2) & 1) + ((p >> 3) ^ ((p >> 2) & 1))) + (p & 3)


def dot(a, b):
    return jnp.dot(a, b, preferred_element_type=F32)


def pick(rows, cols, rule):
    i = lax.broadcasted_iota(jnp.int32, (rows, cols), 0)
    k = lax.broadcasted_iota(jnp.int32, (rows, cols), 1)
    return jnp.where(rule(i, k), 1.0, 0.0).astype(BF)


def kernel(
    res, query, lengths, cache_hbm, wg_hbm, wu_hbm, wd_hbm, wo_hbm, out,
    wgu, wd, wo, cache, xg, xn, st, sg, pb, r1, t2, r2, t3, r3, hid, ctxg, acc, cs, rc, sy, ry, ysum, se, rz,
    qs, qv, qh, cb, csd, crv, lsem, ssem, rsem,
):
    w = lax.axis_index("wide")
    n = lax.axis_index("narrow")
    z, yh, c = w // 4, (w // 2) % 2, w % 2
    yl, x = n // 4, n % 4
    width = res.shape[1] * 8
    half = wg_hbm.shape[1]
    third = half // 3
    wide_tile = 256
    taken = [0]
    pending = []

    place = {"a": ((x + 1) % 4) // 2, "b": x // 2, "y": yl}
    across = {"a": yl * 4 + x + 1 - 2 * (x % 2), "b": yl * 4 + 3 - x, "y": (1 - yl) * 4 + x}

    pw = z * 4 + (1 - yh) * 2 + c
    sw = z * 4 + yh * 2 + (1 - c)
    wplace = {"a": ((z + 1) % 4) // 2, "b": z // 2, "h": yh, "c": c}
    wacross = {"a": (z + 1 - 2 * (z % 2)) * 4 + yh * 2 + c, "b": (3 - z) * 4 + yh * 2 + c, "h": pw, "c": sw}

    def spot(lead, dims, fixed):
        return tuple(lead) + tuple(fixed.get(d, slice(None)) for d in dims)

    def near(k):
        return ((yl + k // 4) % 2) * 4 + (x + k % 4) % 4

    def z_at(d):
        return ((z + d) % 4) * 4 + yh * 2 + c

    def send(src, dst, wt, nt):
        i = taken[0]
        taken[0] += 1
        copy = pltpu.make_async_remote_copy(
            src_ref=src, dst_ref=dst, send_sem=ssem.at[i], recv_sem=rsem.at[i],
            device_id=(wt, nt), device_id_type=MESH,
        )
        copy.start()
        pending.append(copy)
        return copy

    def drain():
        for copy in pending:
            copy.wait_send()
        pending.clear()

    loads = []

    landed = set()

    def load(src, dst):
        copy = pltpu.make_async_copy(src, dst, lsem.at[len(loads)])
        copy.start()
        loads.append(copy)

    def land(copies):
        for copy in copies:
            if id(copy) not in landed:
                landed.add(id(copy))
                copy.wait()

    for g in range(3):
        load(wg_hbm.at[:, pl.ds(g * third, third)], wgu.at[:, pl.ds(2 * g * third, third)])
        load(wu_hbm.at[:, pl.ds(g * third, third)], wgu.at[:, pl.ds((2 * g + 1) * third, third)])

    barrier = pltpu.get_barrier_semaphore()
    for k in range(1, 8):
        pl.semaphore_signal(barrier, inc=1, device_id=(w, near(k)), device_id_type=MESH)
    for peer in (sw, pw, z_at(1), z_at(3), z_at(2)):
        pl.semaphore_signal(barrier, inc=1, device_id=(peer, n), device_id_type=MESH)

    rows_f = res[...].astype(F32)
    total = jnp.sum(rows_f, axis=1, keepdims=True)
    square = jnp.sum(rows_f * rows_f, axis=1, keepdims=True)
    lane = lax.broadcasted_iota(jnp.int32, (32, 128), 1)
    mine = jnp.where(lane < 64, total, square)
    st[0] = mine
    moved = jnp.zeros((256, HEAD), F32)
    for h in range(3):
        table = pick(256, 64, lambda i, k: (whole(i >> 4) == (k >> 2)) & ((i & 15) == 4 * h + (k & 3)))
        moved += dot(table, query[:, h * HEAD:(h + 1) * HEAD])
    qs[...] = moved.astype(BF).reshape(2, 2, 2, 2, 16, HEAD)
    pl.semaphore_wait(barrier, 12)

    turns = {}

    def turn(held, landing, step):
        if step > 0:
            turns[step - 1].wait_recv()
            turns[step - 1].wait_send()
            pending[:] = [copy for copy in pending if copy is not turns[step - 1]]
            d = TURNS[step - 1]
            held[spot((), WIDE, {d: 1 - wplace[d]})] = landing[step - 1]
        if step < 4:
            d = TURNS[step]
            turns[step] = send(held.at[spot((), WIDE, {d: 1 - wplace[d]})], landing.at[step], wacross[d], n)

    stats = [send(st.at[0], st.at[k], w, near(k)) for k in range(1, 8)]
    xg[z, yh, c] = res[...]

    def rows_at(zz, yy):
        return xg.at[zz, yy, c]

    mate = send(rows_at(z, yh), rows_at(z, yh), pw, n)
    first = {d: send(rows_at(z, yh), rows_at(z, yh), z_at(d), n) for d in (1, 3)}
    sib = [send(rows_at(z, yh), rows_at(z, yh), sw, n)]
    second, passed, gathers = {}, {}, {}
    turn(qs, qv, 0)
    load(cache_hbm.at[0], cache)

    def gather(step):
        if step > 0:
            gathers[step - 1].wait_recv()
        if step < 4:
            d = TURNS[step]
            region = sg.at[spot((), WIDE, {e: wplace[e] for e in TURNS[step:]})]
            gathers[step] = send(region, region, wacross[d], n)

    def statistics():
        sums = mine
        for k, copy in enumerate(stats):
            copy.wait_recv()
            sums += st[k + 1]
        mean = sums[:, 0:1] / width
        variance = sums[:, 64:65] / width - mean * mean
        scale = lax.rsqrt(variance + 1e-06)
        row = lax.broadcasted_iota(jnp.int32, (32, 128), 0)
        line = jnp.sum(
            jnp.where(lane == row, mean, 0.0) + jnp.where(lane == row + 32, scale, 0.0), axis=0, keepdims=True
        )
        sg[wplace["a"], wplace["b"], yh, c] = jnp.broadcast_to(line, (8, 128))
        gather(0)

    def normalize(zc):
        row = lax.broadcasted_iota(jnp.int32, (32, 128), 0)
        for h in range(2):
            for k in range(2):
                line = sg[((zc + 1) % 4) // 2, zc // 2, h, k][0:1, :]
                mean = jnp.sum(jnp.where(lane == row, line, 0.0), axis=1, keepdims=True)
                scale = jnp.sum(jnp.where(lane == row + 32, line, 0.0), axis=1, keepdims=True)
                at = (2 * h + k) * 32
                xn[at:at + 32, :] = ((xg[zc, h, k].astype(F32) - mean) * scale).astype(BF)

    def mates():
        mate.wait_recv()
        for d in (1, 3):
            second[d] = send(rows_at(z, 1 - yh), rows_at(z, 1 - yh), z_at(d), n)
        sib.append(send(rows_at(z, 1 - yh), rows_at(z, 1 - yh), sw, n))
        load(wo_hbm, wo)
        load(wd_hbm, wd)

    def onward(d):
        zc = (z + 4 - d) % 4
        first[d].wait_recv()
        if d == 1:
            first[2] = send(rows_at(zc, yh), rows_at(zc, yh), z_at(1), n)
        second[d].wait_recv()
        if d == 3:
            second[2] = send(rows_at(zc, 1 - yh), rows_at(zc, 1 - yh), z_at(3), n)
        passed[d] = send(xg.at[zc, :, c], xg.at[zc, :, c], sw, n)

    def queries_in():
        table = pick(
            192, 256,
            lambda i, k: (i == (k & 3) * 48 + whole(k >> 4) * 3 + ((k >> 2) & 3)) & (((k >> 2) & 3) < 3),
        )
        qh[...] = dot(table, qs[...].reshape(256, HEAD)).astype(BF)
        land(loads[6:7])

    def attend(r):
        scores = lax.dot_general(
            qh[r * 48:(r + 1) * 48, :], cache[r, :, 0:HEAD], (((1,), (1,)), ((), ())),
            preferred_element_type=F32,
        ) * (1.0 / 16.0)
        at = lax.broadcasted_iota(jnp.int32, scores.shape, 1)
        scores = jnp.where(at < lengths[0, r], scores, -jnp.inf)
        top = jnp.max(scores, axis=1, keepdims=True)
        weights = jnp.exp(scores - top)
        probs = (weights / jnp.sum(weights, axis=1, keepdims=True)).astype(BF)
        cb[r * 48:(r + 1) * 48, :] = dot(probs, cache[r, :, HEAD:2 * HEAD]).astype(BF)

    contexts = {}

    def context_out():
        table = pick(
            256, 192,
            lambda k, i: (i == (k & 3) * 48 + whole(k >> 4) * 3 + ((k >> 2) & 3)) & (((k >> 2) & 3) < 3),
        )
        csd[...] = dot(table, cb[...]).astype(BF).reshape(2, 2, 2, 2, 16, HEAD)
        turn(csd, crv, 0)

    def spread(ref, lead, order, step):
        fixed = {d: place[d] for d in order[:3 - step]}
        region = ref.at[spot(lead, DIMS, fixed)]
        return send(region, region, w, across[order[2 - step]])

    def context_in():
        arrived = csd[...].reshape(256, HEAD)
        for h in range(3):
            table = pick(64, 256, lambda i, k: (whole(k >> 4) == (i >> 2)) & ((k & 15) == 4 * h + (i & 3)))
            ctxg[h, place["a"], place["b"], place["y"]] = dot(table, arrived).astype(BF)
            contexts[h, 0] = spread(ctxg, (h,), ORDERS[h], 0)

    def context_on(step):
        for h in range(3):
            contexts[h, step - 1].wait_recv()
            contexts[h, step] = spread(ctxg, (h,), ORDERS[h], step)

    parts, hiddens, cores, ys, zs = {}, {}, {}, {}, {}

    def product(j):
        d = STEPS[j]
        zc = (z + 4 - d) % 4
        for copy in sib if d == 0 else [passed[d]]:
            copy.wait_recv()
        normalize(zc)
        rows = xn[...]
        for g in range(3):
            land(loads[2 * g:2 * g + 2])
            for t in range(0, 2 * third, wide_tile):
                value = dot(rows, wgu[:, 2 * g * third + t:2 * g * third + t + wide_tile])
                pb[j, g, :, :, :, :, t:t + wide_tile] = value.astype(BF).reshape(2, 2, 2, 16, wide_tile)
            one = ORDERS[g][0]
            parts[j, g, 1] = send(
                pb.at[spot((j, g), DIMS, {one: 1 - place[one]})], r1.at[j, g], w, across[one]
            )

    def halved(j):
        for g in range(3):
            one, two, three = ORDERS[g]
            rest = DIMS.replace(one, "")
            parts[j, g, 1].wait_recv()
            there = {two: 1 - place[two]}
            t2[j, g] = (
                pb[spot((j, g), DIMS, {one: place[one], **there})].astype(F32)
                + r1[spot((j, g), rest, there)].astype(F32)
            ).astype(BF)
            parts[j, g, 2] = send(t2.at[j, g], r2.at[j, g], w, across[two])

    def piece(j, g, last):
        one, two, three = ORDERS[g]
        rest = DIMS.replace(one, "")
        fixed = {one: place[one], two: place[two], three: last}
        return (
            pb[spot((j, g), DIMS, fixed)].astype(F32)
            + r1[spot((j, g), rest, fixed)].astype(F32)
            + r2[j, g, last].astype(F32)
        )

    def quartered(j):
        for g in range(3):
            three = ORDERS[g][2]
            parts[j, g, 2].wait_recv()
            t3[j, g] = piece(j, g, 1 - place[three]).astype(BF)
            parts[j, g, 3] = send(t3.at[j, g], r3.at[j, g], w, across[three])

    def hidden(j):
        for g in range(3):
            three = ORDERS[g][2]
            parts[j, g, 3].wait_recv()
            value = piece(j, g, place[three]) + r3[j, g].astype(F32)
            gate, up = value[:, :third], value[:, third:]
            hid[j, g, place["a"], place["b"], place["y"]] = (gate / (1.0 + jnp.exp(-gate)) * up).astype(BF)
            hiddens[j, g, 0] = spread(hid, (j, g), ORDERS[g], 0)

    def hidden_on(j, step):
        for g in range(3):
            hiddens[j, g, step - 1].wait_recv()
            hiddens[j, g, step] = spread(hid, (j, g), ORDERS[g], step)

    def result(j):
        zc = (z + 4 - STEPS[j]) % 4
        land(loads[7:9])
        for h in range(3):
            if contexts.get((h, 2)) is not None:
                contexts.pop((h, 2)).wait_recv()
        for g in range(3):
            hiddens[j, g, 2].wait_recv()
        rows = jnp.concatenate([hid[j, g].reshape(128, third) for g in range(3)], axis=1)
        cb_, cy = zc % 2, zc // 2
        heads = jnp.concatenate([
            jnp.concatenate([ctxg[h, cb_, cb_, cy], ctxg[h, 1 - cb_, cb_, cy]], axis=0) for h in range(3)
        ], axis=1)
        for t in range(0, wd.shape[1], wide_tile):
            cols = slice(t, t + wide_tile)
            value = (dot(rows, wd[:, cols]) + dot(heads, wo[:, cols])).reshape(2, 2, 32, wide_tile)
            acc[j, :, :, cols] = jnp.where(c == 0, value[:, 0], value[:, 1])
            cs[j, :, :, cols] = jnp.where(c == 0, value[:, 1], value[:, 0]).astype(BF)
        cores[j] = send(cs.at[j], rc.at[j], sw, n)

    def core_sum(j):
        d = STEPS[j]
        cores[j].wait_recv()
        sy[j] = (acc[j, 1 - yh] + rc[j, 1 - yh].astype(F32)).astype(BF)
        ys[j] = send(sy.at[j], ry.at[j], pw, n)
        acc[j, yh] += rc[j, yh].astype(F32)

    def y_sum(j):
        d = STEPS[j]
        ys[j].wait_recv()
        value = acc[j, yh] + ry[j].astype(F32)
        if d == 0:
            ysum[...] = value
        else:
            se[j] = value.astype(BF)
            zs[4 - d] = send(se.at[j], rz.at[4 - d], z_at(4 - d), n)

    turn(qs, qv, 1)
    statistics()
    turn(qs, qv, 2)
    gather(1)
    mates()
    turn(qs, qv, 3)
    gather(2)
    product(3)
    onward(3)
    gather(3)
    turn(qs, qv, 4)
    queries_in()
    onward(1)
    attend(0)
    attend(1)
    attend(2)
    attend(3)
    context_out()
    halved(3)
    gather(4)
    turn(csd, crv, 1)
    product(0)
    onward(2)
    product(1)
    turn(csd, crv, 2)
    product(2)
    halved(0)
    quartered(3)
    turn(csd, crv, 3)
    halved(1)
    halved(2)
    quartered(0)
    turn(csd, crv, 4)
    context_in()
    quartered(1)
    hidden(3)
    quartered(2)
    hidden(0)
    context_on(1)
    hidden(1)
    hidden_on(3, 1)
    hidden_on(0, 1)
    hidden(2)
    context_on(2)
    hidden_on(1, 1)
    hidden_on(0, 2)
    hidden_on(2, 1)
    hidden_on(1, 2)
    result(0)
    hidden_on(3, 2)
    hidden_on(2, 2)
    result(1)
    core_sum(0)
    core_sum(1)
    result(2)
    result(3)
    core_sum(2)
    y_sum(0)
    y_sum(1)
    core_sum(3)
    y_sum(2)
    drain()
    y_sum(3)

    value = ysum[...]
    for e in (3, 1, 2):
        zs[e].wait_recv()
        value += rz[e].astype(F32)
    out[...] = value.astype(BF)
    drain()


def local(residual_in, query, cache, lengths, gate_weight, up_weight, down_weight, out_weight):
    rows, width = residual_in.shape
    half = gate_weight.shape[1]
    cols = query.shape[1]
    places = cache.shape[2]
    vmem = pl.BlockSpec(memory_space=pltpu.VMEM)
    hbm = pl.BlockSpec(memory_space=pl.ANY)
    copies = 176
    return pl.pallas_call(
        kernel,
        out_shape=jax.ShapeDtypeStruct((rows, width), BF),
        in_specs=[vmem, vmem, pl.BlockSpec(memory_space=pltpu.SMEM), hbm, hbm, hbm, hbm, hbm],
        out_specs=vmem,
        scratch_shapes=[
            pltpu.VMEM((width, 2 * half), BF),
            pltpu.VMEM((half, width), BF),
            pltpu.VMEM((cols, width), BF),
            pltpu.VMEM((4, places, 2 * HEAD), BF),
            pltpu.VMEM((4, 2, 2, 32, width), BF),
            pltpu.VMEM((128, width), BF),
            pltpu.VMEM((8, 32, 128), F32),
            pltpu.VMEM((2, 2, 2, 2, 8, 128), F32),
            pltpu.VMEM((4, 3, 2, 2, 2, 16, 2 * half // 3), BF),
            pltpu.VMEM((4, 3, 2, 2, 16, 2 * half // 3), BF),
            pltpu.VMEM((4, 3, 2, 16, 2 * half // 3), BF),
            pltpu.VMEM((4, 3, 2, 16, 2 * half // 3), BF),
            pltpu.VMEM((4, 3, 16, 2 * half // 3), BF),
            pltpu.VMEM((4, 3, 16, 2 * half // 3), BF),
            pltpu.VMEM((4, 3, 2, 2, 2, 16, half // 3), BF),
            pltpu.VMEM((3, 2, 2, 2, 64, HEAD), BF),
            pltpu.VMEM((4, 2, 32, width), F32),
            pltpu.VMEM((4, 2, 32, width), BF),
            pltpu.VMEM((4, 2, 32, width), BF),
            pltpu.VMEM((4, 32, width), BF),
            pltpu.VMEM((4, 32, width), BF),
            pltpu.VMEM((32, width), F32),
            pltpu.VMEM((4, 32, width), BF),
            pltpu.VMEM((4, 32, width), BF),
            pltpu.VMEM((2, 2, 2, 2, 16, HEAD), BF),
            pltpu.VMEM((4, 2, 2, 2, 16, HEAD), BF),
            pltpu.VMEM((192, HEAD), BF),
            pltpu.VMEM((192, HEAD), BF),
            pltpu.VMEM((2, 2, 2, 2, 16, HEAD), BF),
            pltpu.VMEM((4, 2, 2, 2, 16, HEAD), BF),
            pltpu.SemaphoreType.DMA((9,)),
            pltpu.SemaphoreType.DMA((copies,)),
            pltpu.SemaphoreType.DMA((copies,)),
        ],
        compiler_params=pltpu.CompilerParams(
            collective_id=0, has_side_effects=True, vmem_limit_bytes=58 << 20
        ),
        name="layer",
    )(residual_in, query, lengths, cache, gate_weight, up_weight, down_weight, out_weight)


def solution(mesh):
    return jax.shard_map(
        local,
        mesh=mesh,
        in_specs=(
            P("wide", "narrow"),
            P("narrow", "wide"),
            P("narrow", "wide", None, None),
            P("narrow", "wide"),
            P("narrow", "wide"),
            P("narrow", "wide"),
            P("wide", "narrow"),
            P("wide", "narrow"),
        ),
        out_specs=P("wide", "narrow"),
        check_vma=False,
    )
```

time: 342 us -> 82.8 us (0.24)
  blocking collectives: 139 us -> 0 us
  waiting for transfers between devices: 137 us -> 0 us
  Pallas kernels: 0 us -> 81.1 us
  matrix products: 30.5 us -> 0 us
  between operations: 13.2 us -> 0.01 us
  local copies, waits for them, and re-layouts: 9.77 us -> 1.58 us
  other arithmetic: 7.46 us -> 0 us
  starting transfers between devices: 4.24 us -> 0 us
    all_gather x1 -> x0, blocking collectives: 86.2 us -> none  [local(): lax.all_gather(context_local, 'narrow', axis=0, tiled=True)]
    reduce_scatter x1 -> x0, waiting for transfers between devices: 81.5 us -> none  [local(): lax.psum_scatter(ffn_part, 'wide', scatter_dimension=0, tiled=True)]
    pallas_call x0 -> x1, Pallas kernels: none -> 81.1 us  [local(): pl.pallas_call(kernel, out_shape=jax.ShapeDtypeStruct((rows, width), BF),...]
    all_gather x1 -> x0, waiting for transfers between devices: 48.2 us -> none  [local(): piece = lax.all_gather(normed, 'wide', axis=0, tiled=True)]
    all_to_all x1 -> x0, blocking collectives: 33.2 us -> none  [local(): lax.all_to_all(context, 'wide', split_axis=1, concat_axis=0, tiled=True)]
    dot_general x6 -> x0, matrix products: 30.5 us -> none  [the longest x1 6.98 us: local(): ffn_part = jnp.dot(hidden, down_weight, preferred_element_type=jnp.float32)]
    psum x1 -> x0, blocking collectives: 19.8 us -> none  [local(): lax.psum((jnp.sum(rows_f, axis=1), jnp.sum(rows_f * rows_f, axis=1)), 'na...]
    all_to_all x1 -> x0, waiting for transfers between devices: 7.69 us -> none  [local(): lax.all_to_all(query, 'wide', split_axis=0, concat_axis=1, tiled=True)]
  transfers between devices with their start and end apart: 4 -> 0, of which waited for: 3 -> 0; matrix products, arithmetic and copies ran while one was open for 3% -> 0% of each run, Pallas kernels for 0% -> 0%
where the time goes in v2:
time: 82.8 us; the launch traced here: 82.7 us
  Pallas kernels  81.1 us (98%)
  local copies, waits for them, and re-layouts  1.58 us (2%)
    pallas_call x1, Pallas kernels, local(): pl.pallas_call(kernel, out_shape=jax.ShapeDtypeStruct((rows, width), BF),...  81.1 us

profile of v2, /device:TPU:0, one launch (start us, length us, event | category | flops | bytes accessed | tf_op | source)
XLA Modules:
  0.0 82.7 jit_solution(13358542788818359881)
XLA Ops:
  0.0 81.1 %layer.1 = bf16[32,2304]{1,0:T(8,128)(2,1)} custom-call(bf16[32,2304]{1,0:T(8,128)(2,1)} %res.1, bf16[64,768]{1,0:T(8,128)(2,1)} %query.1, s32[1,4]{1,0:T(1,128)} %lengths.1, bf16[1,4,1536,512]{3,2,1,0:T(8,128)(2,1)} %cache_hbm.1, bf16[2304,1152]{1,0:T(8,128)(2,1)} %wg_hbm.1, bf16[2304,1152]{1,0:T(8,128)(2,1)} %wu_hbm.1, bf16[1152,2304]{1,0:T(8,128)(2,1)} %wd_hbm.1, ...), custom_call_target="tpu_custom_call" | custom-call | tf_op jit(solution)/shard_map/layer/pallas_call | solution.py:424
  81.1 1.6 %copy.10 = bf16[32,2304]{1,0:T(8,128)(2,1)} copy(bf16[32,2304]{1,0:T(8,128)(2,1)} %layer.1) | data formatting | bytes 294912

commit v3 on v2

--- a/solution.py
+++ b/solution.py
@@ -11,6 +11,7 @@
 BF = jnp.bfloat16
 F32 = jnp.float32
 STEPS = (1, 3, 2, 0)
+Z_FIRST = (1, 3)
 DIMS = "aby"
 ORDERS = ("aby", "bya", "yab")
 WIDE = "abhc"
@@ -33,7 +34,7 @@
 
 def kernel(
     res, query, lengths, cache_hbm, wg_hbm, wu_hbm, wd_hbm, wo_hbm, out,
-    wgu, wd, wo, cache, xg, xn, st, sg, pb, r1, t2, r2, t3, r3, hid, ctxg, acc, cs, rc, sy, ry, ysum, se, rz,
+    wgu, wd, wo, cache, xg, xn, st, sg, pb, r1, t2, r2, t3, r3, hid, ctxg, acc, cs, rc, sy, ry, ysum, se, rz, sz, rzz,
     qs, qv, qh, cb, csd, crv, lsem, ssem, rsem,
 ):
     w = lax.axis_index("wide")
@@ -75,10 +76,11 @@
         pending.append(copy)
         return copy
 
-    def drain():
-        for copy in pending:
+    def drain(keep=0):
+        done = len(pending) - keep
+        for copy in pending[:done]:
             copy.wait_send()
-        pending.clear()
+        del pending[:done]
 
     loads = []
 
@@ -104,6 +106,8 @@
         pl.semaphore_signal(barrier, inc=1, device_id=(w, near(k)), device_id_type=MESH)
     for peer in (sw, pw, z_at(1), z_at(3), z_at(2)):
         pl.semaphore_signal(barrier, inc=1, device_id=(peer, n), device_id_type=MESH)
+
+    xg[z, yh, c] = res[...]
 
     rows_f = res[...].astype(F32)
     total = jnp.sum(rows_f, axis=1, keepdims=True)
@@ -111,11 +115,6 @@
     lane = lax.broadcasted_iota(jnp.int32, (32, 128), 1)
     mine = jnp.where(lane < 64, total, square)
     st[0] = mine
-    moved = jnp.zeros((256, HEAD), F32)
-    for h in range(3):
-        table = pick(256, 64, lambda i, k: (whole(i >> 4) == (k >> 2)) & ((i & 15) == 4 * h + (k & 3)))
-        moved += dot(table, query[:, h * HEAD:(h + 1) * HEAD])
-    qs[...] = moved.astype(BF).reshape(2, 2, 2, 2, 16, HEAD)
     pl.semaphore_wait(barrier, 12)
 
     turns = {}
@@ -131,16 +130,20 @@
             d = TURNS[step]
             turns[step] = send(held.at[spot((), WIDE, {d: 1 - wplace[d]})], landing.at[step], wacross[d], n)
 
-    stats = [send(st.at[0], st.at[k], w, near(k)) for k in range(1, 8)]
-    xg[z, yh, c] = res[...]
 
     def rows_at(zz, yy):
         return xg.at[zz, yy, c]
 
     mate = send(rows_at(z, yh), rows_at(z, yh), pw, n)
     first = {d: send(rows_at(z, yh), rows_at(z, yh), z_at(d), n) for d in (1, 3)}
+    stats = [send(st.at[0], st.at[k], w, near(k)) for k in range(1, 8)]
     sib = [send(rows_at(z, yh), rows_at(z, yh), sw, n)]
     second, passed, gathers = {}, {}, {}
+    moved = jnp.zeros((256, HEAD), F32)
+    for h in range(3):
+        table = pick(256, 64, lambda i, k: (whole(i >> 4) == (k >> 2)) & ((i & 15) == 4 * h + (k & 3)))
+        moved += dot(table, query[:, h * HEAD:(h + 1) * HEAD])
+    qs[...] = moved.astype(BF).reshape(2, 2, 2, 2, 16, HEAD)
     turn(qs, qv, 0)
     load(cache_hbm.at[0], cache)
 
@@ -327,9 +330,20 @@
     def core_sum(j):
         d = STEPS[j]
         cores[j].wait_recv()
-        sy[j] = (acc[j, 1 - yh] + rc[j, 1 - yh].astype(F32)).astype(BF)
+        if d in Z_FIRST:
+            sz[j] = (acc[j] + rc[j].astype(F32)).astype(BF)
+            zs[4 - d] = send(sz.at[j], rzz.at[4 - d], z_at(4 - d), n)
+            return
+        there = acc[j, 1 - yh] + rc[j, 1 - yh].astype(F32)
+        here = acc[j, yh] + rc[j, yh].astype(F32)
+        if d == 0:
+            for e in Z_FIRST:
+                zs[4 - e].wait_recv()
+                there += rzz[4 - e, 1 - yh].astype(F32)
+                here += rzz[4 - e, yh].astype(F32)
+        sy[j] = there.astype(BF)
         ys[j] = send(sy.at[j], ry.at[j], pw, n)
-        acc[j, yh] += rc[j, yh].astype(F32)
+        acc[j, yh] = here
 
     def y_sum(j):
         d = STEPS[j]
@@ -344,16 +358,16 @@
     turn(qs, qv, 1)
     statistics()
     turn(qs, qv, 2)
+    mates()
     gather(1)
-    mates()
     turn(qs, qv, 3)
     gather(2)
     product(3)
     onward(3)
     gather(3)
+    onward(1)
     turn(qs, qv, 4)
     queries_in()
-    onward(1)
     attend(0)
     attend(1)
     attend(2)
@@ -376,39 +390,38 @@
     turn(csd, crv, 4)
     context_in()
     quartered(1)
-    hidden(3)
     quartered(2)
     hidden(0)
     context_on(1)
     hidden(1)
-    hidden_on(3, 1)
+    hidden(3)
     hidden_on(0, 1)
     hidden(2)
+    hidden_on(1, 1)
     context_on(2)
-    hidden_on(1, 1)
+    hidden_on(2, 1)
     hidden_on(0, 2)
-    hidden_on(2, 1)
+    hidden_on(3, 1)
     hidden_on(1, 2)
+    hidden_on(2, 2)
     result(0)
-    hidden_on(3, 2)
-    hidden_on(2, 2)
     result(1)
+    result(2)
     core_sum(0)
     core_sum(1)
-    result(2)
+    hidden_on(3, 2)
+    core_sum(2)
     result(3)
-    core_sum(2)
-    y_sum(0)
-    y_sum(1)
+    y_sum(2)
+    drain(10)
     core_sum(3)
-    y_sum(2)
-    drain()
     y_sum(3)
 
     value = ysum[...]
-    for e in (3, 1, 2):
-        zs[e].wait_recv()
-        value += rz[e].astype(F32)
+    for d in (1, 3, 2):
+        if d not in Z_FIRST:
+            zs[4 - d].wait_recv()
+            value += rz[4 - d].astype(F32)
     out[...] = value.astype(BF)
     drain()
 
@@ -451,6 +464,8 @@
             pltpu.VMEM((32, width), F32),
             pltpu.VMEM((4, 32, width), BF),
             pltpu.VMEM((4, 32, width), BF),
+            pltpu.VMEM((4, 2, 32, width), BF),
+            pltpu.VMEM((4, 2, 32, width), BF),
             pltpu.VMEM((2, 2, 2, 2, 16, HEAD), BF),
             pltpu.VMEM((4, 2, 2, 2, 16, HEAD), BF),
             pltpu.VMEM((192, HEAD), BF),

time: 82.8 us -> 81.2 us (0.981)
  Pallas kernels: 81.1 us -> 79.4 us
    pallas_call x1, Pallas kernels: 81.1 us -> 79.4 us  [local(): pl.pallas_call(kernel, out_shape=jax.ShapeDtypeStruct((rows, width), BF),...]
where the time goes in v3:
time: 81.2 us; the launch traced here: 81 us
  Pallas kernels  79.4 us (98%)
  local copies, waits for them, and re-layouts  1.58 us (2%)
    pallas_call x1, Pallas kernels, local(): pl.pallas_call(kernel, out_shape=jax.ShapeDtypeStruct((rows, width), BF),...  79.4 us

profile of v3, /device:TPU:0, one launch (start us, length us, event | category | flops | bytes accessed | tf_op | source)
XLA Modules:
  0.0 81.0 jit_solution(11336928462252493115)
XLA Ops:
  0.0 79.4 %layer.1 = bf16[32,2304]{1,0:T(8,128)(2,1)} custom-call(bf16[32,2304]{1,0:T(8,128)(2,1)} %res.1, bf16[64,768]{1,0:T(8,128)(2,1)} %query.1, s32[1,4]{1,0:T(1,128)} %lengths.1, bf16[1,4,1536,512]{3,2,1,0:T(8,128)(2,1)} %cache_hbm.1, bf16[2304,1152]{1,0:T(8,128)(2,1)} %wg_hbm.1, bf16[2304,1152]{1,0:T(8,128)(2,1)} %wu_hbm.1, bf16[1152,2304]{1,0:T(8,128)(2,1)} %wd_hbm.1, ...), custom_call_target="tpu_custom_call" | custom-call | tf_op jit(solution)/shard_map/layer/pallas_call | solution.py:437
  79.4 1.6 %copy.10 = bf16[32,2304]{1,0:T(8,128)(2,1)} copy(bf16[32,2304]{1,0:T(8,128)(2,1)} %layer.1) | data formatting | bytes 294912
